TPU v7x, 256 devices: a whole 4x4x8 slice. The times are simulated.
256 devices in a mesh: tile: 32 (over y, z_hi, core), trc: 8 (over x, z_lo).
Axes of the slice: x: 4, y: 4, z: 8 (z_hi: 4, z_lo: 2; z = z_hi * 2 + z_lo), core: 2. Of those that a mesh axis runs over, the one named last changes fastest.
Arguments:
- tracers: float32 [64, 48, 256, 256], P('trc', None, 'tile'), may hold values from -6 to 6
- archive: bfloat16 [8, 4, 48, 256, 256], P('trc', None, None, 'tile'), may hold values from -0.14941406 to 0.14941406
- sea_mask: int32 [256, 256], P('tile'), may hold values 0 or 1
- levels: int32 [256, 256], P('tile'), may hold values from 1 to 48
Outputs:
- transported: float32 [64, 48, 256, 256], P('trc', None, 'tile')
All inputs are finite; a program needn't handle non-finite values. No bound on the sum of `sea_mask` on one device may be relied on, other than what follows from the above.
Results may differ from a plain program's by a relative error of at most 0.00055.
Values may be sent and summed in bfloat16 or wider, within the bound.
A program may use at most 64 MiB of HBM per device.

v0:
```python
import jax
import jax.numpy as jnp
from jax import lax
from jax.sharding import PartitionSpec as P

STEPS = 3


DIFFUSION = 0.04
MIX_SCALE = 0.3


def spread(value, axis, source):
    kept = jnp.where(lax.axis_index(axis) == source, value, 0).astype(value.dtype)
    return lax.psum(kept, axis)


def as_sent(shard):

    def short(part):
        return part.astype(jnp.bfloat16) if part.dtype == jnp.float32 else part

    return jax.tree.map(short, shard)


def from_behind(shard, axis, by):
    length = lax.axis_size(axis)
    return lax.ppermute(shard, axis, [(i, (i + by) % length) for i in range(length)])


def face_flux(left_vals, right_vals, left_wet, right_wet, courant):
    moved = jnp.maximum(courant, 0.0) * left_vals + jnp.minimum(courant, 0.0) * right_vals
    return (moved + DIFFUSION * (left_vals - right_vals)) * (left_wet * right_wet)


def inner_change(tracer, wetness, fields):
    merid = fields[1][:, :, 1:]
    south = tracer[..., :-1]
    north = tracer[..., 1:]
    northward = face_flux(south, north, wetness[:, :, :-1], wetness[:, :, 1:], merid)
    edge = jnp.zeros_like(northward[..., :1])
    padded = jnp.concatenate([edge, northward, edge], axis=-1)
    merid_change = padded[..., :-1] - padded[..., 1:]
    upward = fields[2][1:]
    mixing = MIX_SCALE * jnp.abs(fields[3][1:])
    above = tracer[..., :-1, :, :]
    below = tracer[..., 1:, :, :]
    moved = jnp.maximum(upward, 0.0) * below + jnp.minimum(upward, 0.0) * above
    rising = (moved + mixing * (below - above)) * (wetness[:-1] * wetness[1:])
    edge_v = jnp.zeros_like(rising[..., :1, :, :])
    padded_v = jnp.concatenate([edge_v, rising, edge_v], axis=-3)
    vert_change = padded_v[..., 1:, :, :] - padded_v[..., :-1, :, :]
    return (merid_change, vert_change)


def fetch_record(archive, turn_index):
    record = spread(archive[0], "trc", turn_index % lax.axis_size("trc"))
    return record.astype(jnp.float32)


def zonal_part(tracer, wetness, zonal):
    groups = tracer.shape[0]
    west_rim = jnp.concatenate([tracer[:, :, -1, :], wetness[None, :, -1, :]], axis=0)
    arrived = from_behind(as_sent(west_rim), "tile", 1).astype(west_rim.dtype)
    west_vals = jnp.concatenate([arrived[:groups, :, None, :], tracer[:, :, :-1, :]], axis=2)
    west_wet = jnp.concatenate([arrived[groups][:, None, :], wetness[:, :-1, :]], axis=1)
    eastward = face_flux(west_vals, tracer, west_wet, wetness, zonal)
    beyond = from_behind(as_sent(eastward[:, :, 0, :]), "tile", -1)
    east_side = jnp.concatenate([eastward[:, :, 1:, :], beyond[:, :, None, :]], axis=2)
    return eastward - east_side


def per_device(tracers, archive, sea_mask, levels):
    depth = tracers.shape[1]
    level_ids = jnp.arange(depth, dtype=jnp.int32)[:, None, None]
    wetness = (sea_mask[None] * (level_ids < levels[None]).astype(jnp.int32)).astype(jnp.float32)
    current = tracers
    for turn_index in range(STEPS):
        fields = fetch_record(archive, turn_index)
        zonal_change = zonal_part(current, wetness, fields[0])
        merid_change, vert_change = inner_change(current, wetness, fields)
        current = current + zonal_change + merid_change + vert_change
    return current


def solution(mesh):
    in_specs = (
        P("trc", None, "tile", None),
        P("trc", None, None, "tile", None),
        P("tile", None),
        P("tile", None),
    )
    out_specs = P("trc", None, "tile", None)
    return jax.shard_map(
        per_device, mesh=mesh, in_specs=in_specs, out_specs=out_specs, check_vma=False
    )
```

profile of v0, /device:TPU:32, one launch (start us, length us, event | category | flops | bytes accessed | tf_op | source)
XLA Modules:
  0.0 208.6 jit_solution(15363983279671680484)
XLA Ops:
  6.5 2.6 %select_bitcast_fusion = (bf16[4,48,8,256]{3,2,1,0:T(8,128)(2,1)}, bf16[4,48,8,256]{3,2,1,0:T(8,128)(2,1)}, bf16[4,48,8,256]{3,2,1,0:T(8,128)(2,1)}) fusion(bf16[1,4,48,8,256]{4,3,2,1,0:T(8,128)(2,1)} %param.5, pred[]{:T(512)S(6)} %eq.11, pred[]{:T(512)S(6)} %eq.9, pred[]{:T(512)S(6)} %eq.10), kind=kLoop, calls=%fused_computation.24 | loop fusion | flops 1179648 | bytes 3145731 | tf_op jit(solution)/shard_map/jit(_where)/select_n | solution.py:14
  9.2 2.9 %copy.48 = f32[8,48,8,256]{3,1,0,2:T(8,128)S(1)} copy(f32[8,48,8,256]{3,2,1,0:T(8,128)} %param.4) | data formatting | bytes 6291456 | tf_op args[0]
  12.2 0.6 copy-done.9
  12.9 0.9 copy-done
  13.8 0.2 slice_multiply_fusion.1
  14.0 12.2 %collective-permute-done = bf16[9,48,256]{2,1,0:T(8,128)(2,1)S(1)} collective-permute-done((bf16[9,48,256]{2,1,0:T(8,128)(2,1)S(1)}, bf16[9,48,256]{2,1,0:T(8,128)(2,1)S(1)}, u32[]{:S(2)}, u32[]{:S(2)}) %collective-permute-start) | collective-permute-done | bytes 221216 | tf_op jit(solution)/shard_map/ppermute | solution.py:28
  26.3 105.7 %all-reduce.15.cloned.1.call-done = (bf16[4,48,8,256]{3,2,1,0:T(8,128)(2,1)}, bf16[4,48,8,256]{3,2,1,0:T(8,128)(2,1)}, bf16[4,48,8,256]{3,2,1,0:T(8,128)(2,1)}) async-done(((bf16[4,48,8,256]{3,2,1,0:T(8,128)(2,1)}, bf16[4,48,8,256]{3,2,1,0:T(8,128)(2,1)}, bf16[4,48,8,256]{3,2,1,0:T(8,128)(2,1)}), (bf16[4,48,8,256]{3,2,1,0:T(8,128)(2,1)}, bf16[4,48,8,256]{3,2,1,0:T(8,128)(2,1)}, ...) | async-done | bytes 2359312 | tf_op jit(solution)/shard_map/psum | solution.py:15
  132.0 1.4 convert_element_type.69
  133.7 0.1 copy.42
  133.8 0.1 copy.45
  133.9 0.2 copy-done.2
  134.2 1.2 slice-done
  135.4 1.6 add_multiply_fusion.8
  137.0 1.7 copy-done.8
  138.7 0.1 convert_element_type.75
  139.0 0.1 copy.53
  139.2 0.1 copy.55
  139.3 0.1 copy.57
  139.5 6.0 %collective-permute-start.1 = (bf16[8,48,256]{2,1,0:T(8,128)(2,1)S(1)}, bf16[8,48,256]{2,1,0:T(8,128)(2,1)S(1)}, u32[]{:S(2)}, u32[]{:S(2)}) collective-permute-start(bf16[8,48,256]{2,1,0:T(8,128)(2,1)S(1)} %fusion.19), channel_id=1, source_target_pairs={{0,248},{8,0},{16,8},{24,16},{32,24},{40,32},{48,40},{56,48},{64,5... | collective-permute-start | bytes 589832 | tf_op jit(solution)/shard_map/ppermute | solution.py:28
  145.5 0.2 slice_maximum_fusion.2
  145.6 0.1 copy.49
  145.8 0.1 copy.51
  145.9 0.2 slice_maximum_fusion.1
  146.1 0.1 copy.60
  146.2 0.1 copy.61
  146.4 0.1 copy.62
  146.5 0.1 copy.63
  146.6 0.1 copy.64
  146.8 0.1 copy.58
  146.9 0.1 copy.59
  147.1 0.1 convert_element_type.80
  147.3 0.2 slice_maximum_fusion
  147.5 0.1 copy.67
  147.6 0.1 copy.68
  147.7 1.2 copy-done.1
  148.9 1.0 add_multiply_fusion.7
  149.9 1.3 add_multiply_fusion.6
  151.3 0.1 copy.69
  151.5 0.1 copy.70
  151.6 0.1 copy.71
  151.7 0.1 copy.65
  151.9 0.1 copy.66
  152.1 1.0 copy-done.4
  153.1 0.8 slice-done.1
  154.0 3.6 %fusion.2 = f32[8,48,8,256]{3,1,0,2:T(8,128)S(1)} fusion(f32[8,48,8,256]{3,1,0,2:T(8,128)S(1)} %copy-done.4, f32[8,48,1,256]{3,1,0,2:T(8,128)S(1)} %bitcast_convert_fusion.2, f32[8,48,7,256]{3,1,0,2:T(8,128)S(1)} %slice-done.1, f32[8,47,8,256]{3,1,0,2:T(8,128)S(1)} %add_multiply_fusion.6, f32[8,48,8,255]{3,1,0,2:T(8,128)S(1)} %add_multiply_fusion.7, ...), kind=kLoop, calls=%fused_computation.4 | loop fusion | flops 5505024 | bytes 18796544 | tf_op jit(solution)/shard_map/add | solution.py:82
  157.6 0.2 slice.288
  157.8 0.5 copy-done.10
  158.4 1.2 add_multiply_fusion.3
  159.6 10.7 %collective-permute-done.2 = bf16[9,48,256]{2,1,0:T(8,128)(2,1)S(1)} collective-permute-done((bf16[9,48,256]{2,1,0:T(8,128)(2,1)S(1)}, bf16[9,48,256]{2,1,0:T(8,128)(2,1)S(1)}, u32[]{:S(2)}, u32[]{:S(2)}) %collective-permute-start.2) | collective-permute-done | bytes 221216 | tf_op jit(solution)/shard_map/ppermute | solution.py:28
  170.5 1.0 add_multiply_fusion.5
  171.5 0.3 collective-permute-start.3
  171.8 0.9 add_multiply_fusion.4
  172.8 0.2 slice.290
  173.0 2.0 collective-permute-done.3
  175.1 3.0 %fusion.5 = f32[8,48,8,256]{3,1,0,2:T(8,128)S(1)} fusion(f32[8,48,8,256]{3,1,0,2:T(8,128)S(1)} %fusion.2, f32[8,48,8,256]{3,1,0,2:T(8,128)S(1)} %add_multiply_fusion.5, f32[8,48,1,256]{3,1,0,2:T(8,128)S(1)} %bitcast_convert_fusion.1, f32[8,48,7,256]{3,1,0,2:T(8,128)S(1)} %slice.290, f32[8,47,8,256]{3,1,0,2:T(8,128)S(1)} %add_multiply_fusion.3, ...), kind=kLoop, calls=%fused_computation.9 | loop fusion | flops 5505024 | bytes 18796544 | tf_op jit(solution)/shard_map/add | solution.py:82
  178.1 0.2 slice.303
  178.6 1.2 add_multiply_fusion
  179.7 11.0 %collective-permute-done.4 = bf16[9,48,256]{2,1,0:T(8,128)(2,1)S(1)} collective-permute-done((bf16[9,48,256]{2,1,0:T(8,128)(2,1)S(1)}, bf16[9,48,256]{2,1,0:T(8,128)(2,1)S(1)}, u32[]{:S(2)}, u32[]{:S(2)}) %collective-permute-start.4) | collective-permute-done | bytes 221216 | tf_op jit(solution)/shard_map/ppermute | solution.py:28
  190.8 1.0 add_multiply_fusion.2
  192.0 0.9 add_multiply_fusion.1
  192.9 0.2 slice.305
  193.2 2.0 collective-permute-done.5
  195.3 3.0 %fusion.8 = f32[8,48,8,256]{3,1,0,2:T(8,128)S(1)} fusion(f32[8,48,8,256]{3,1,0,2:T(8,128)S(1)} %fusion.5, f32[8,48,8,256]{3,1,0,2:T(8,128)S(1)} %add_multiply_fusion.2, f32[8,48,1,256]{3,1,0,2:T(8,128)S(1)} %bitcast_convert_fusion, f32[8,48,7,256]{3,1,0,2:T(8,128)S(1)} %slice.305, f32[8,47,8,256]{3,1,0,2:T(8,128)S(1)} %add_multiply_fusion, ...), kind=kLoop, calls=%fused_computation.14 | loop fusion | flops 5505024 | bytes 18796544 | tf_op jit(solution)/shard_map/add | solution.py:82
  198.3 3.4 %copy.72 = f32[8,48,8,256]{3,2,1,0:T(8,128)} copy(f32[8,48,8,256]{3,1,0,2:T(8,128)S(1)} %fusion.8) | data formatting | bytes 6291456 | tf_op jit(solution)/shard_map/add | solution.py:82
  (62 shorter events, 1.6 us)
Async XLA Ops:
  6.5 125.5 %all-reduce.15.cloned.1.call-start = ((), (), s32[]{:S(2)}) async-start(), calls=%async_computation | async-start | bytes 4718592 | tf_op jit(solution)/shard_map/psum | solution.py:15
  9.1 2.9 %copy-start.11 = (s32[8,256]{1,0:T(8,128)S(1)}, s32[8,256]{1,0:T(8,128)}, u32[]{:S(2)}) copy-start(s32[8,256]{1,0:T(8,128)} %param.6) | copy-start | bytes 24580
  9.2 2.9 %copy-start.12 = (s32[8,256]{1,0:T(8,128)S(1)}, s32[8,256]{1,0:T(8,128)}, u32[]{:S(2)}) copy-start(s32[8,256]{1,0:T(8,128)} %param.7) | copy-start | bytes 24580
  12.1 1.7 copy-start
  12.2 0.7 copy-start.9
  12.9 13.3 %collective-permute-start = (bf16[9,48,256]{2,1,0:T(8,128)(2,1)S(1)}, bf16[9,48,256]{2,1,0:T(8,128)(2,1)S(1)}, u32[]{:S(2)}, u32[]{:S(2)}) collective-permute-start(bf16[9,48,256]{2,1,0:T(8,128)(2,1)S(1)} %pad_maximum_fusion.8), channel_id=1, source_target_pairs={{0,8},{8,16},{16,24},{24,32},{32,40},{40,48},{48,56},{56,64},{64,7... | collective-permute-start | bytes 663560 | tf_op jit(solution)/shard_map/ppermute | solution.py:28
  12.9 13.3 %copy-start.5 = (f32[48,7,256]{2,0,1:T(8,128)}, f32[48,7,256]{2,0,1:T(8,128)S(1)}, u32[]{:S(2)}) copy-start(f32[48,7,256]{2,0,1:T(8,128)S(1)} %slice.270) | copy-start | bytes 1032196
  132.0 2.1 %copy-start.2 = (f32[8,48,8,256]{3,2,1,0:T(8,128)S(1)}, f32[8,48,8,256]{3,2,1,0:T(8,128)}, u32[]{:S(2)}) copy-start(f32[8,48,8,256]{3,2,1,0:T(8,128)} %param.4) | copy-start | bytes 9437188
  133.5 2.0 slice-start
  137.0 1.9 copy-start.3
  137.0 1.7 copy-start.8
  139.5 12.6 %collective-permute-start.1 = (bf16[8,48,256]{2,1,0:T(8,128)(2,1)S(1)}, bf16[8,48,256]{2,1,0:T(8,128)(2,1)S(1)}, u32[]{:S(2)}, u32[]{:S(2)}) collective-permute-start(bf16[8,48,256]{2,1,0:T(8,128)(2,1)S(1)} %fusion.19), channel_id=1, source_target_pairs={{0,248},{8,0},{16,8},{24,16},{32,24},{40,32},{48,40},{56,48},{64,5... | collective-permute-start | bytes 589832 | tf_op jit(solution)/shard_map/ppermute | solution.py:28
  145.9 1.1 copy-start.7
  147.0 1.9 copy-start.1
  151.2 1.9 copy-start.4
  151.2 2.7 %slice-start.1 = ((f32[8,48,8,256]{3,1,0,2:T(8,128)}), f32[8,48,7,256]{3,1,0,2:T(8,128)S(1)}, s32[]{:S(2)}) async-start(f32[8,48,8,256]{3,1,0,2:T(8,128)} %copy-done.3), calls=%async_computation.2 | async-start | bytes 5505024 | tf_op jit(solution)/shard_map/slice | solution.py:69
  157.6 0.7 copy-start.10
  158.3 12.1 %copy-start.6 = (f32[48,7,256]{2,0,1:T(8,128)S(1)}, f32[48,7,256]{2,0,1:T(8,128)}, u32[]{:S(2)}) copy-start(f32[48,7,256]{2,0,1:T(8,128)} %copy-done.5) | copy-start | bytes 1032196
  158.3 12.0 %collective-permute-start.2 = (bf16[9,48,256]{2,1,0:T(8,128)(2,1)S(1)}, bf16[9,48,256]{2,1,0:T(8,128)(2,1)S(1)}, u32[]{:S(2)}, u32[]{:S(2)}) collective-permute-start(bf16[9,48,256]{2,1,0:T(8,128)(2,1)S(1)} %pad_maximum_fusion.7), channel_id=1, source_target_pairs={{0,8},{8,16},{16,24},{24,32},{32,40},{40,48},{48,56},{56,64},{64,7... | collective-permute-start | bytes 663560 | tf_op jit(solution)/shard_map/ppermute | solution.py:28
  171.5 3.5 %collective-permute-start.3 = (bf16[8,48,256]{2,1,0:T(8,128)(2,1)S(1)}, bf16[8,48,256]{2,1,0:T(8,128)(2,1)S(1)}, u32[]{:S(2)}, u32[]{:S(2)}) collective-permute-start(bf16[8,48,256]{2,1,0:T(8,128)(2,1)S(1)} %fusion.21), channel_id=1, source_target_pairs={{0,248},{8,0},{16,8},{24,16},{32,24},{40,32},{48,40},{56,48},{64,5... | collective-permute-start | bytes 589832 | tf_op jit(solution)/shard_map/ppermute | solution.py:28
  178.5 12.2 %collective-permute-start.4 = (bf16[9,48,256]{2,1,0:T(8,128)(2,1)S(1)}, bf16[9,48,256]{2,1,0:T(8,128)(2,1)S(1)}, u32[]{:S(2)}, u32[]{:S(2)}) collective-permute-start(bf16[9,48,256]{2,1,0:T(8,128)(2,1)S(1)} %pad_maximum_fusion.6), channel_id=1, source_target_pairs={{0,8},{8,16},{16,24},{24,32},{32,40},{40,48},{48,56},{56,64},{64,7... | collective-permute-start | bytes 663560 | tf_op jit(solution)/shard_map/ppermute | solution.py:28
  191.9 3.3 %collective-permute-start.5 = (bf16[8,48,256]{2,1,0:T(8,128)(2,1)S(1)}, bf16[8,48,256]{2,1,0:T(8,128)(2,1)S(1)}, u32[]{:S(2)}, u32[]{:S(2)}) collective-permute-start(bf16[8,48,256]{2,1,0:T(8,128)(2,1)S(1)} %fusion.23), channel_id=1, source_target_pairs={{0,248},{8,0},{16,8},{24,16},{32,24},{40,32},{48,40},{56,48},{64,5... | collective-permute-start | bytes 589832 | tf_op jit(solution)/shard_map/ppermute | solution.py:28
Sparse Core Ops, SparseCore 0:
  10.2 121.7 all-reduce.14
where the time goes:
time: 210 us; the launch traced here: 209 us
  waiting for transfers between devices  144 us (69%)
  other arithmetic  25.7 us (12%)
  local copies, waits for them, and re-layouts  18.6 us (9%)
  between operations  14.2 us (7%)
  starting transfers between devices  6.55 us (3%)
    psum x1, waiting for transfers between devices, spread(): return lax.psum(kept, axis)  106 us
    ppermute x6, waiting for transfers between devices, from_behind(): lax.ppermute(shard, axis, [(i, (i + by) % length) for i in range(length)])  37.9 us
    add x3, other arithmetic, per_device(): current = current + zonal_change + merid_change + vert_change  9.69 us
    unnamed x27, local copies, waits for them, and re-layouts  9.09 us
    ppermute x6, starting transfers between devices, from_behind(): lax.ppermute(shard, axis, [(i, (i + by) % length) for i in range(length)])  6.55 us
    mul x6, other arithmetic, face_flux(): (moved + DIFFUSION * (left_vals - right_vals)) * (left_wet * right_wet)  6.4 us
  transfers between devices with their start and end apart: 7, of which 6 were waited for; matrix products, arithmetic and copies ran while one was open for 6% of the time, Pallas kernels for 0%

commit v1 on v0

v1 whole, which is shorter than its diff:
```python
import functools

import jax
import jax.numpy as jnp
from jax import lax
from jax.experimental import pallas as pl
from jax.experimental.pallas import tpu as pltpu
from jax.sharding import PartitionSpec as P

MESH = pl.DeviceIdType.MESH
STEPS = 3
DIFFUSION = 0.04
MIX_SCALE = 0.3
TRACERS, LEV, LON, LAT = 8, 48, 8, 256
ROWS = LEV * LON
PAIRS = LEV // 2
TILES, GROUP = 32, 8

EVENTS = (
    (3, 99, 195, 96, 197, 100, 6, 98),
    (14, 107, 207, 201, 201, 195, 10, 104),
    (17, 113, 230, 105, 0, 201, 192, 122),
    (192, 122, 0, 113, 213, 108, 30, 3),
    (26, 11, 211, 225, 10, 122, 200, 8),
    (41, 130, 17, 9, 17, 117, 38, 134),
    (200, 139, 41, 137, 26, 211, 208, 192),
    (34, 147, 235, 194, 45, 0, 50, 26),
    (51, 155, 52, 145, 98, 8, 20, 136),
    (208, 1, 217, 50, 34, 130, 56, 201),
    (59, 192, 250, 124, 217, 43, 40, 148),
    (226, 162, 61, 152, 48, 140, 86, 35),
    (65, 177, 258, 210, 107, 26, 131, 112),
    (232, 200, 8, 0, 56, 144, 221, 154),
    (73, 170, 65, 59, 69, 34, 90, 208),
    (82, 187, 266, 128, 114, 225, 105, 17),
    (254, 50, 24, 181, 82, 156, 226, 166),
    (91, 251, 77, 75, 73, 56, 145, 41),
    (258, 32, 275, 26, 88, 67, 64, 174),
    (266, 208, 32, 188, 237, 162, 250, 83),
    (276, 17, 92, 40, 137, 177, 72, 50),
    (129, 58, 282, 248, 128, 170, 262, 225),
    (286, 275, 98, 91, 120, 73, 162, 217),
    (216, 40, 123, 32, 224, 234, 232, 186),
    (98, 24, 104, 17, 245, 48, 270, 65),
    (104, 81, 241, 64, 154, 89, 137, 56),
    (122, 72, 80, 272, 248, 80, 96, 176),
    (145, 281, 128, 160, 273, 16, 171, 259),
    (176, 224, 179, 80, 162, 243, 241, 250),
    (114, 88, 114, 168, 177, 184, 120, 72),
    (137, 64, 187, 281, 256, 248, 272, 274),
    (184, 217, 145, 234, 185, 256, 282, 267),
    (168, 257, 154, 240, 170, 281, 176, 88),
    (154, 265, 162, 217, 144, 264, 112, 241),
    (240, 234, 136, 256, 264, 272, 184, 280),
    (160, 240, 168, 264, 280, 216, 152, 232),
)
READY = ((14, 28, 24, 26, 31, 33), (27, 34, 35, 36, 36, 35), (14, 36, 36, 36, 36, 36))
SLABS = 6
AHEAD = 1
PIECES = SLABS * 2
SLAB_ROWS = ROWS // SLABS
SLAB_PAIRS = PAIRS // SLABS
EARLY = 6
VMEM_LIMIT = 48 * 2**20


def batch(j):
    low = 0 if j == 0 else SLAB_PAIRS * j - 1
    high = PAIRS if j == SLABS - 1 else SLAB_PAIRS * (j + 1) - 1
    return low, high


def by_rank(rank, values):
    total = jnp.int32(values[0])
    for r in range(1, GROUP):
        if values[r] != values[0]:
            total = jnp.where(rank == r, jnp.int32(values[r]), total)
    return total


def kernel(
    tracers, archive, sea_mask_hbm, levels_hbm, out,
    cur_a, cur_b, rec, rim_out, rim_in, halo, edge, masks, zonal_own, zrim_out, zrim_in, zrim, wet_out, wet_in, sea_mask, levels,
    load_sem, piece_send, piece_recv, rim_send, rim_recv, zrim_send, zrim_recv, wet_send, wet_recv, store_sem,
):
    tile = lax.axis_index("tile")
    rank = lax.axis_index("trc")
    x, z = rank // 2, rank % 2
    beside = (
        lax.rem(x + 1, 4) * 2 + z,
        lax.rem(x + 3, 4) * 2 + z,
        x * 2 + 1 - z,
    )
    east, west = lax.rem(tile + 1, TILES), lax.rem(tile + TILES - 1, TILES)

    first = pltpu.make_async_copy(tracers, cur_a.at[:, pl.ds(8, ROWS)], load_sem.at[0])
    own = pltpu.make_async_copy(archive.at[0], zonal_own, load_sem.at[1])

    def piece_ref(ref, record, half, slab):
        rows = pl.ds(pl.multiple_of(slab * SLAB_ROWS, SLAB_ROWS), SLAB_ROWS)
        if record is None:
            return ref.at[pl.ds(2 * half, 2), rows]
        return ref.at[record, pl.ds(2 * half, 2), rows]

    for r in range(STEPS):
        @pl.when(rank == r)
        def _():
            for j in range(SLABS):
                for h in range(2):
                    pltpu.make_async_copy(
                        piece_ref(archive, None, h, j), piece_ref(rec, r, h, j), piece_recv.at[r * PIECES + 2 * j + h]
                    ).start()

    own.start()
    maps = [
        pltpu.make_async_copy(src, dst, load_sem.at[2 + i])
        for i, (src, dst) in enumerate(((sea_mask_hbm, sea_mask), (levels_hbm, levels)))
    ]
    for c in maps:
        c.start()
    first.start()

    barrier = pltpu.get_barrier_semaphore()
    for k in range(1, GROUP):
        pl.semaphore_signal(barrier, inc=1, device_id={"trc": lax.rem(rank + k, GROUP)}, device_id_type=MESH)
    for n in (east, west):
        pl.semaphore_signal(barrier, inc=1, device_id={"tile": n}, device_id_type=MESH)

    row = lax.broadcasted_iota(jnp.int32, (2, LON, LAT), 1)
    lane = lax.broadcasted_iota(jnp.int32, (LON, LAT), 1)
    level_of = lax.broadcasted_iota(jnp.int32, (3, LON, LAT), 0)
    row_a = row[0]

    for c in maps:
        c.wait()
    depth = sea_mask[...] * levels[...]
    wet_out[...] = depth.astype(jnp.float32)
    for ref in (cur_a, cur_b):
        for t in range(TRACERS):
            ref[t, pl.ds(0, 8)] = jnp.zeros((8, LAT), jnp.float32)
            ref[t, pl.ds(ROWS + 8, 8)] = jnp.zeros((8, LAT), jnp.float32)
    pl.semaphore_wait(barrier, GROUP + 1)

    def tile_copy(src, dst, send, recv, to):
        return pltpu.make_async_remote_copy(
            src_ref=src, dst_ref=dst, send_sem=send, recv_sem=recv, device_id={"tile": to}, device_id_type=MESH
        )

    wet_copies = [
        tile_copy(wet_out, wet_in.at[side], wet_send.at[side], wet_recv.at[side], to)
        for side, to in ((0, east), (1, west))
    ]
    for c in wet_copies:
        c.start()

    words = []
    for e in range(0, len(EVENTS), 3):
        words.append(
            by_rank(rank, [sum(EVENTS[e + i][r] << (9 * i) for i in range(3)) for r in range(GROUP)])
        )

    def event_parts(e):
        code = (words[e // 3] // (1 << (9 * (e % 3)))) % 512
        return code // 8, code % 8

    def hand_on(p, d):
        ref = piece_ref(rec, p // PIECES, p % 2, (p % PIECES) // 2)
        return pltpu.make_async_remote_copy(
            src_ref=ref, dst_ref=ref, send_sem=piece_send.at[p, d], recv_sem=piece_recv.at[p],
            device_id={"trc": beside[d]}, device_id_type=MESH,
        )

    def event(e):
        p, dirs = event_parts(e)
        ref = piece_ref(rec, p // PIECES, p % 2, (p % PIECES) // 2)
        pltpu.make_async_copy(ref, ref, piece_recv.at[p]).wait()
        for d in range(3):
            if any((v >> d) & 1 for v in EVENTS[e]):
                @pl.when((dirs // (1 << d)) % 2 == 1)
                def _():
                    hand_on(p, d).start()

    def rim_copies(s, j):
        low, high = batch(j)
        rows = pl.ds(16 * low, 16 * (high - low))
        return [
            tile_copy(
                rim_out.at[s, side, rows], rim_in.at[s, side, rows], rim_send.at[s, side, j], rim_recv.at[s, side, j], to
            )
            for side, to in ((0, east), (1, west))
        ]

    def put_edges(t, value):
        for k in range(2):
            edge[0, pl.ds(2 * t + k, 1)] = value[k, 7:8]
            edge[1, pl.ds(2 * t + k, 1)] = value[k, 0:1]

    def put_rims(s, start):
        for side in range(2):
            rim_out[s, side, pl.ds(start, 16)] = edge[side].astype(jnp.bfloat16)

    def early_events():
        for e in range(EARLY):
            event(e)

    @pl.when(rank == 0)
    def _():
        early_events()

    def zrim_west(r):
        return tile_copy(zrim_out, zrim_in.at[r], zrim_send.at[0], zrim_recv.at[r], west)

    def zrim_round(r, k):
        return pltpu.make_async_remote_copy(
            src_ref=zrim_in.at[r], dst_ref=zrim_in.at[r], send_sem=zrim_send.at[k], recv_sem=zrim_recv.at[r],
            device_id={"trc": lax.rem(rank + k, GROUP)}, device_id_type=MESH,
        )

    own.wait()
    for g in range(LEV // 16):
        for q in range(8):
            value = zonal_own[pl.ds(128 * g + 16 * q, 16)].astype(jnp.float32).reshape(2, LON, LAT)
            for k in range(2):
                edge[0, pl.ds(2 * q + k, 1)] = value[k, 0:1]
        zrim_out[pl.ds(16 * g, 16)] = edge[0].astype(jnp.bfloat16)
    for r in range(STEPS):
        @pl.when(rank == r)
        def _():
            zrim_west(r).start()

    first.wait()
    for j in range(SLABS):
        low, high = batch(j)

        def first_rims(p, _):
            start = pl.multiple_of(16 * p, 16)
            for t in range(TRACERS):
                put_edges(t, cur_a[t, pl.ds(start + 8, 16)].reshape(2, LON, LAT))
            put_rims(0, start)
            return 0

        lax.fori_loop(low, high, first_rims, 0)
        for c in rim_copies(0, j):
            c.start()

    @pl.when(rank != 0)
    def _():
        early_events()

    for r in range(STEPS):
        @pl.when(rank == r)
        def _():
            zrim_west(r).wait_recv()
            for k in range(1, GROUP):
                zrim_round(r, k).start()

    for c in wet_copies:
        c.wait()
    depth_w, depth_e = wet_in[0, 7:8], wet_in[1, 0:1]
    depth_f = depth.astype(jnp.float32)
    beyond_w = jnp.where(row_a == 0, depth_w, pltpu.roll(depth_f, 1, 0))
    beyond_e = jnp.where(row_a == LON - 1, depth_e, pltpu.roll(depth_f, LON - 1, 0))
    beyond_s = jnp.where(lane == 0, 0.0, pltpu.roll(depth_f, 1, 1))
    beyond_n = jnp.where(lane == LAT - 1, 0.0, pltpu.roll(depth_f, LAT - 1, 1))
    for i, beyond in enumerate((beyond_w, beyond_e, beyond_s, beyond_n)):
        masks[i] = jnp.minimum(depth_f, beyond)
    masks[4] = depth_f

    def work(s, j, source, target):
        low, high = batch(j)
        for c in rim_copies(s, j):
            c.wait_recv()

        def pair(p, _):
            start = pl.multiple_of(16 * p, 16)
            after = pl.multiple_of(16 * p + 16, 16)
            level3 = (level_of + 2 * p).astype(jnp.float32)
            level2 = level3[:2]

            def field(f, at):
                return rec[s, f, pl.ds(at, 16)].astype(jnp.float32).reshape(2, LON, LAT)

            def two_sided(courant, mask):
                plus = jnp.maximum(courant, 0.0) + DIFFUSION
                wet = mask[None] > level2
                return jnp.where(wet, plus, 0.0), jnp.where(wet, plus - courant, 0.0)

            zonal = field(0, start)
            zonal_e = pltpu.roll(zonal, LON - 1, 1)
            rims = [jnp.broadcast_to(zrim[pl.ds(2 * p + k, 1)], (LON, LAT)) for k in range(2)]
            zonal_e = jnp.where(row == LON - 1, jnp.stack(rims), zonal_e)
            from_w, to_w = two_sided(zonal, masks[0])
            to_e, from_e = two_sided(zonal_e, masks[1])
            merid = field(1, start)
            from_s, to_s = two_sided(merid, masks[2])
            to_n, from_n = two_sided(pltpu.roll(merid, LAT - 1, 2), masks[3])
            upward = jnp.concatenate([field(2, start), field(2, after)[:1]], axis=0)
            mixing = MIX_SCALE * jnp.abs(jnp.concatenate([field(3, start), field(3, after)[:1]], axis=0))
            wet3 = jnp.logical_and(masks[4][None] > level3, level3 > 0.0)
            plus3 = jnp.maximum(upward, 0.0) + mixing
            lower = jnp.where(wet3, plus3, 0.0)
            upper = jnp.where(wet3, plus3 - upward, 0.0)
            from_below, to_above = lower[1:], lower[:2]
            from_above, to_below = upper[:2], upper[1:]
            stay = 1.0 - (to_w + to_e + to_s + to_n + to_above + to_below)

            for side in range(2):
                halo[side] = rim_in[s, side, pl.ds(start, 16)].astype(jnp.float32)
            for t in range(TRACERS):
                four = source[t, pl.ds(start, 32)].reshape(4, LON, LAT)
                here = four[1:3]
                side_w = jnp.stack([jnp.broadcast_to(halo[0, pl.ds(2 * t + k, 1)], (LON, LAT)) for k in range(2)])
                side_e = jnp.stack([jnp.broadcast_to(halo[1, pl.ds(2 * t + k, 1)], (LON, LAT)) for k in range(2)])
                at_w = jnp.where(row == 0, side_w, pltpu.roll(here, 1, 1))
                at_e = jnp.where(row == LON - 1, side_e, pltpu.roll(here, LON - 1, 1))
                new = stay * here + from_w * at_w + from_e * at_e
                new += from_s * pltpu.roll(here, 1, 2) + from_n * pltpu.roll(here, LAT - 1, 2)
                new += from_below * four[2:4] + from_above * four[0:2]
                target[t, pl.ds(pl.multiple_of(start + 8, 8), 16)] = new.reshape(16, LAT)
                if s < STEPS - 1:
                    put_edges(t, new)
            if s < STEPS - 1:
                put_rims(s + 1, start)
            return 0

        lax.fori_loop(low, high, pair, 0)
        if s < STEPS - 1:
            for c in rim_copies(s + 1, j):
                c.start()

    done = EARLY
    stores = []
    for s in range(STEPS):
        source, target = ((cur_a, cur_b), (cur_b, cur_a))[s % 2]
        for j in range(SLABS):
            upto = READY[s][j]
            if s < STEPS - 1 or j < SLABS - 1:
                upto = min(len(EVENTS), upto + AHEAD)
            for e in range(done, upto):
                event(e)
            done = max(done, upto)
            if j == 0:
                @pl.when(rank != s)
                def _():
                    zrim_west(s).wait_recv()
                zrim[...] = zrim_in[s].astype(jnp.float32)
            work(s, j, source, target)
            if s == STEPS - 1:
                low, high = batch(j)
                count = 16 * (high - low)
                c = pltpu.make_async_copy(
                    target.at[:, pl.ds(8 + 16 * low, count)], out.at[:, pl.ds(16 * low, count)], store_sem.at[j]
                )
                c.start()
                stores.append(c)

    for s in range(STEPS):
        for j in range(SLABS):
            for c in rim_copies(s, j):
                c.wait_send()
    for r in range(STEPS):
        @pl.when(rank == r)
        def _():
            zrim_west(r).wait_send()
            for k in range(1, GROUP):
                zrim_round(r, k).wait_send()
    for e in range(len(EVENTS)):
        p, dirs = event_parts(e)
        for d in range(3):
            if any((v >> d) & 1 for v in EVENTS[e]):
                @pl.when((dirs // (1 << d)) % 2 == 1)
                def _():
                    hand_on(p, d).wait_send()
    for c in stores:
        c.wait()


def per_device(tracers, archive, sea_mask, levels):
    any_space = pl.BlockSpec(memory_space=pl.ANY)
    in_hbm = pl.BlockSpec(memory_space=pltpu.HBM)
    dma = pltpu.SemaphoreType.DMA
    result = pl.pallas_call(
        kernel,
        out_shape=jax.ShapeDtypeStruct((TRACERS, ROWS, LAT), jnp.float32),
        in_specs=[in_hbm, in_hbm, in_hbm, in_hbm],
        out_specs=any_space,
        scratch_shapes=[
            pltpu.VMEM((TRACERS, ROWS + 16, LAT), jnp.float32),
            pltpu.VMEM((TRACERS, ROWS + 16, LAT), jnp.float32),
            pltpu.VMEM((STEPS, 4, ROWS + 16, LAT), jnp.bfloat16),
            pltpu.VMEM((STEPS, 2, ROWS, LAT), jnp.bfloat16),
            pltpu.VMEM((STEPS, 2, ROWS, LAT), jnp.bfloat16),
            pltpu.VMEM((2, 16, LAT), jnp.float32),
            pltpu.VMEM((2, 16, LAT), jnp.float32),
            pltpu.VMEM((5, LON, LAT), jnp.float32),
            pltpu.VMEM((ROWS, LAT), jnp.bfloat16),
            pltpu.VMEM((LEV, LAT), jnp.bfloat16),
            pltpu.VMEM((STEPS, LEV, LAT), jnp.bfloat16),
            pltpu.VMEM((LEV, LAT), jnp.float32),
            pltpu.VMEM((LON, LAT), jnp.float32),
            pltpu.VMEM((2, LON, LAT), jnp.float32),
            pltpu.VMEM((LON, LAT), jnp.int32),
            pltpu.VMEM((LON, LAT), jnp.int32),
            dma((4,)),
            dma((STEPS * PIECES, 3)),
            dma((STEPS * PIECES,)),
            dma((STEPS, 2, SLABS)),
            dma((STEPS, 2, SLABS)),
            dma((GROUP,)),
            dma((STEPS,)),
            dma((2,)),
            dma((2,)),
            dma((SLABS,)),
        ],
        compiler_params=pltpu.CompilerParams(
            collective_id=0, has_side_effects=True, vmem_limit_bytes=VMEM_LIMIT
        ),
    )(
        tracers.reshape(TRACERS, ROWS, LAT),
        archive.reshape(4, ROWS, LAT),
        sea_mask,
        levels,
    )
    return result.reshape(TRACERS, LEV, LON, LAT)


def solution(mesh):
    in_specs = (
        P("trc", None, "tile", None),
        P("trc", None, None, "tile", None),
        P("tile", None),
        P("tile", None),
    )
    return jax.shard_map(
        per_device, mesh=mesh, in_specs=in_specs, out_specs=P("trc", None, "tile", None), check_vma=False
    )
```

time: 210 us -> 62.3 us (0.30)
  waiting for transfers between devices: 144 us -> 0 us
  Pallas kernels: 0 us -> 57.8 us
  other arithmetic: 25.7 us -> 0 us
  local copies, waits for them, and re-layouts: 18.6 us -> 4.19 us
  between operations: 14.2 us -> 0.01 us
  starting transfers between devices: 6.55 us -> 0 us
    psum x1 -> x0, waiting for transfers between devices: 106 us -> none  [spread(): return lax.psum(kept, axis)]
    pallas_call x0 -> x1, Pallas kernels: none -> 57.8 us  [per_device(): pl.pallas_call(kernel, out_shape=jax.ShapeDtypeStruct((TRACERS, ROWS, LAT...]
    ppermute x6 -> x0, waiting for transfers between devices: 37.9 us -> none  [from_behind(): lax.ppermute(shard, axis, [(i, (i + by) % length) for i in range(length)])]
    mul x17 -> x0, other arithmetic: 10.7 us -> none  [the longest x6 6.4 us: face_flux(): (moved + DIFFUSION * (left_vals - right_vals)) * (left_wet * right_wet)]
    add x3 -> x0, other arithmetic: 9.69 us -> none  [per_device(): current = current + zonal_change + merid_change + vert_change]
    ppermute x6 -> x0, starting transfers between devices: 6.55 us -> none  [from_behind(): lax.ppermute(shard, axis, [(i, (i + by) % length) for i in range(length)])]
    unnamed x27 -> x7, local copies, waits for them, and re-layouts: 9.09 us -> 4.19 us
    add x1 -> x0, local copies, waits for them, and re-layouts: 3.45 us -> none  [per_device(): current = current + zonal_change + merid_change + vert_change]
  transfers between devices with their start and end apart: 7 -> 0, of which waited for: 6 -> 0; matrix products, arithmetic and copies ran while one was open for 6% -> 0% of each run, Pallas kernels for 0% -> 0%
where the time goes in v1:
time: 62.3 us; the launch traced here: 62.1 us
  Pallas kernels  57.8 us (93%)
  local copies, waits for them, and re-layouts  4.19 us (7%)
    pallas_call x1, Pallas kernels, per_device(): pl.pallas_call(kernel, out_shape=jax.ShapeDtypeStruct((TRACERS, ROWS, LAT...  57.8 us
    unnamed x7, local copies, waits for them, and re-layouts  4.19 us

profile of v1, /device:TPU:32, one launch (start us, length us, event | category | flops | bytes accessed | tf_op | source)
XLA Modules:
  0.0 62.1 jit_solution(4061033809188509303)
XLA Ops:
  0.0 0.0 copy-start
  0.0 1.1 %copy-done = bf16[1,4,48,8,256]{4,3,2,1,0:T(8,128)(2,1)S(1)} copy-done((bf16[1,4,48,8,256]{4,3,2,1,0:T(8,128)(2,1)S(1)}, bf16[1,4,48,8,256]{4,3,2,1,0:T(8,128)(2,1)}, u32[]{:S(2)}) %copy-start) | copy-done | bytes 786456
  1.1 0.0 copy-start.1
  1.1 0.7 %copy-done.1 = s32[8,256]{1,0:T(8,128)S(1)} copy-done((s32[8,256]{1,0:T(8,128)S(1)}, s32[8,256]{1,0:T(8,128)}, u32[]{:S(2)}) %copy-start.1) | copy-done | bytes 8216
  1.8 0.0 copy-start.2
  1.8 0.7 %copy-done.2 = s32[8,256]{1,0:T(8,128)S(1)} copy-done((s32[8,256]{1,0:T(8,128)S(1)}, s32[8,256]{1,0:T(8,128)}, u32[]{:S(2)}) %copy-start.2) | copy-done | bytes 8216
  2.5 57.8 %shard_map.46 = f32[8,384,256]{2,1,0:T(8,128)S(1)} custom-call(f32[8,384,256]{2,1,0:T(8,128)} %bitcast.5, bf16[4,384,256]{2,1,0:T(8,128)(2,1)S(1)} %bitcast.4, s32[8,256]{1,0:T(8,128)S(1)} %copy-done.1, s32[8,256]{1,0:T(8,128)S(1)} %copy-done.2), custom_call_target="tpu_custom_call" | custom-call | tf_op jit(solution)/shard_map/pallas_call | solution.py:382
  60.4 1.7 %copy.6 = f32[8,48,8,256]{3,2,1,0:T(8,128)} copy(f32[8,48,8,256]{3,2,1,0:T(8,128)S(1)} %bitcast.3) | data formatting | bytes 6291456
Async XLA Ops:
  0.0 1.1 %copy-start = (bf16[1,4,48,8,256]{4,3,2,1,0:T(8,128)(2,1)S(1)}, bf16[1,4,48,8,256]{4,3,2,1,0:T(8,128)(2,1)}, u32[]{:S(2)}) copy-start(bf16[1,4,48,8,256]{4,3,2,1,0:T(8,128)(2,1)} %param.5) | copy-start | bytes 2359300
  1.1 0.7 %copy-start.1 = (s32[8,256]{1,0:T(8,128)S(1)}, s32[8,256]{1,0:T(8,128)}, u32[]{:S(2)}) copy-start(s32[8,256]{1,0:T(8,128)} %sea_mask_hbm.1) | copy-start | bytes 24580
  1.8 0.7 %copy-start.2 = (s32[8,256]{1,0:T(8,128)S(1)}, s32[8,256]{1,0:T(8,128)}, u32[]{:S(2)}) copy-start(s32[8,256]{1,0:T(8,128)} %levels_hbm.1) | copy-start | bytes 24580

commit v2 on v1

v2 whole, which is shorter than its diff:
```python
import functools

import jax
import jax.numpy as jnp
from jax import lax
from jax.experimental import pallas as pl
from jax.experimental.pallas import tpu as pltpu
from jax.sharding import PartitionSpec as P

MESH = pl.DeviceIdType.MESH
STEPS = 3
DIFFUSION = 0.04
MIX_SCALE = 0.3
TRACERS, LEV, LON, LAT = 8, 48, 8, 256
HALF = LAT // 2
ROWS = LEV * LON
PAIRS = LEV // 2
TILES, GROUP = 32, 8

EVENTS = (
    (3, 1539, 3075, 1540, 3077, 1540, 6, 1542),
    (131, 1667, 3203, 1668, 3205, 3075, 134, 1670),
    (259, 1795, 3331, 1796, 3333, 1668, 262, 1798),
    (387, 1923, 3459, 1924, 3461, 3203, 390, 1926),
    (3076, 2051, 4, 1, 0, 1796, 1537, 1),
    (515, 2179, 3587, 2052, 3589, 3331, 3072, 2054),
    (3204, 2307, 132, 129, 128, 1924, 518, 129),
    (643, 3072, 3715, 2180, 3717, 3459, 1665, 2182),
    (3332, 2435, 260, 257, 256, 0, 3200, 257),
    (771, 3200, 3843, 2308, 3845, 2052, 646, 2310),
    (3460, 2563, 388, 385, 384, 3587, 1793, 385),
    (899, 3328, 1536, 3072, 1536, 128, 3328, 3072),
    (3588, 2691, 3971, 2436, 3973, 2180, 774, 2438),
    (1027, 3456, 516, 513, 512, 3715, 1921, 513),
    (3716, 2819, 1664, 3200, 1664, 256, 3456, 3200),
    (1155, 0, 4099, 2564, 4101, 2308, 902, 2566),
    (3844, 3584, 644, 641, 640, 3843, 2049, 641),
    (1283, 2947, 1792, 3328, 1792, 384, 3584, 3328),
    (1536, 128, 4227, 2692, 4229, 2436, 1030, 2694),
    (3972, 3712, 772, 769, 768, 3971, 2177, 769),
    (1411, 256, 1920, 3456, 1920, 512, 3712, 3456),
    (1664, 3840, 4355, 2820, 4357, 2564, 1158, 2822),
    (4100, 384, 900, 897, 896, 4099, 2305, 897),
    (1792, 3968, 2048, 3584, 2048, 640, 3840, 3584),
    (4228, 512, 4483, 2948, 4485, 2692, 1286, 2950),
    (1920, 4096, 1028, 1025, 1024, 4227, 2433, 1025),
    (4356, 640, 2176, 3712, 2176, 768, 3968, 3712),
    (2048, 4224, 1156, 1153, 1152, 2820, 1414, 1153),
    (4484, 768, 2304, 3840, 2304, 4355, 2561, 3840),
    (2176, 4352, 1284, 1281, 1280, 896, 4096, 1281),
    (2304, 896, 2432, 3968, 2432, 2948, 2689, 3968),
    (2432, 4480, 1412, 1409, 1408, 4483, 4224, 1409),
    (2560, 1024, 2560, 4096, 2560, 1024, 2817, 4096),
    (2688, 1152, 2688, 4224, 2688, 1152, 4352, 4224),
    (2816, 1280, 2816, 4352, 2816, 1280, 2945, 4352),
    (2944, 1408, 2944, 4480, 2944, 1408, 4480, 4480),
)
READY = ((19, 23, 27, 31, 34, 36), (22, 26, 30, 32, 34, 36), (15, 21, 27, 31, 34, 36))
SLABS = 6
AHEAD = 1
WAYS = ((1, 0), (3, 0), (0, 1), (2, 0), (1, 1), (3, 1), (2, 1))
PIECES = SLABS * 2
SLAB_ROWS = ROWS // SLABS
SLAB_PAIRS = PAIRS // SLABS
EARLY = 6
RELAY = 8
GROUPS = LEV // 8
RIM_ROWS = 8 * TRACERS
VMEM_LIMIT = 48 * 2**20


def batch(j):
    low = 0 if j == 0 else SLAB_PAIRS * j - 1
    high = PAIRS if j == SLABS - 1 else SLAB_PAIRS * (j + 1) - 1
    return low, high


def by_rank(rank, values):
    total = jnp.int32(values[0])
    for r in range(1, GROUP):
        if values[r] != values[0]:
            total = jnp.where(rank == r, jnp.int32(values[r]), total)
    return total


def kernel(
    tracers, archive, sea_mask_hbm, levels_hbm, out,
    cur_a, cur_b, rec, rim_out, rim_in, halo, zonal_f, masks, zonal_own, zrim_out, zrim_in, zrim, wet_out, wet_in, sea_mask, levels,
    load_sem, piece_send, piece_recv, rim_send, rim_recv, zrim_send, zrim_recv, wet_send, wet_recv, store_sem,
):
    tile = lax.axis_index("tile")
    rank = lax.axis_index("trc")
    x, z = rank // 2, rank % 2
    beside = [lax.rem(x + dx, 4) * 2 + lax.rem(z + dz, 2) for dx, dz in WAYS]
    east, west = lax.rem(tile + 1, TILES), lax.rem(tile + TILES - 1, TILES)

    first = [
        pltpu.make_async_copy(
            tracers.at[:, :, pl.ds(HALF * h, HALF)], cur_a.at[h, :, pl.ds(8, ROWS)], load_sem.at[(0, 4)[h]]
        )
        for h in range(2)
    ]
    own = pltpu.make_async_copy(archive.at[0], zonal_own, load_sem.at[1])

    def piece_ref(ref, record, half, slab):
        rows = pl.ds(pl.multiple_of(slab * SLAB_ROWS, SLAB_ROWS), SLAB_ROWS)
        if record is None:
            return ref.at[pl.ds(2 * half, 2), rows]
        return ref.at[record, pl.ds(2 * half, 2), rows]

    for r in range(STEPS):
        @pl.when(rank == r)
        def _():
            for j in range(SLABS):
                for h in range(2):
                    pltpu.make_async_copy(
                        piece_ref(archive, None, h, j), piece_ref(rec, r, h, j), piece_recv.at[r * PIECES + 2 * j + h]
                    ).start()

    @pl.when(rank < STEPS)
    def _():
        own.start()

    maps = [
        pltpu.make_async_copy(src, dst, load_sem.at[2 + i])
        for i, (src, dst) in enumerate(((sea_mask_hbm, sea_mask), (levels_hbm, levels)))
    ]
    for c in maps:
        c.start()
    for c in first:
        c.start()

    barrier = pltpu.get_barrier_semaphore()
    for k in range(1, GROUP):
        pl.semaphore_signal(barrier, inc=1, device_id={"trc": lax.rem(rank + k, GROUP)}, device_id_type=MESH)
    for n in (east, west):
        pl.semaphore_signal(barrier, inc=1, device_id={"tile": n}, device_id_type=MESH)

    row = lax.broadcasted_iota(jnp.int32, (2, LON, LAT), 1)
    lane = lax.broadcasted_iota(jnp.int32, (LON, LAT), 1)
    level_of = lax.broadcasted_iota(jnp.int32, (3, LON, LAT), 0)
    row_a = row[0]

    for c in maps:
        c.wait()
    depth = sea_mask[...] * levels[...]
    wet_out[...] = depth.astype(jnp.float32)
    for ref in (cur_a, cur_b):
        for h in range(2):
            for t in range(TRACERS):
                ref[h, t, pl.ds(0, 8)] = jnp.zeros((8, HALF), jnp.float32)
                ref[h, t, pl.ds(ROWS + 8, 8)] = jnp.zeros((8, HALF), jnp.float32)
    pl.semaphore_wait(barrier, GROUP + 1)

    def tile_copy(src, dst, send, recv, to):
        return pltpu.make_async_remote_copy(
            src_ref=src, dst_ref=dst, send_sem=send, recv_sem=recv, device_id={"tile": to}, device_id_type=MESH
        )

    wet_copies = [
        tile_copy(wet_out, wet_in.at[side], wet_send.at[side], wet_recv.at[side], to)
        for side, to in ((0, east), (1, west))
    ]
    for c in wet_copies:
        c.start()

    words = []
    for e in range(0, len(EVENTS), 2):
        words.append(by_rank(rank, [EVENTS[e][r] + (EVENTS[e + 1][r] << 14) for r in range(GROUP)]))

    def event_parts(e):
        code = words[e // 2] % (1 << 14) if e % 2 == 0 else words[e // 2] // (1 << 14)
        return code // 128, code % 128

    def hand_on(p, d):
        ref = piece_ref(rec, p // PIECES, p % 2, (p % PIECES) // 2)
        return pltpu.make_async_remote_copy(
            src_ref=ref, dst_ref=ref, send_sem=piece_send.at[p, d], recv_sem=piece_recv.at[p],
            device_id={"trc": beside[d]}, device_id_type=MESH,
        )

    def event(e):
        p, dirs = event_parts(e)
        ref = piece_ref(rec, p // PIECES, p % 2, (p % PIECES) // 2)
        pltpu.make_async_copy(ref, ref, piece_recv.at[p]).wait()
        for d in range(len(WAYS)):
            if any((v >> d) & 1 for v in EVENTS[e]):
                @pl.when((dirs // (1 << d)) % 2 == 1)
                def _():
                    hand_on(p, d).start()

    def rim_copies(s, g):
        rows = pl.ds(RIM_ROWS * g, RIM_ROWS)
        return [
            tile_copy(
                rim_out.at[s, side, rows], rim_in.at[s, side, rows], rim_send.at[s, side, g], rim_recv.at[s, side, g], to
            )
            for side, to in ((0, east), (1, west))
        ]

    def send_rims(s, g, ref):
        for side, lon in ((0, LON - 1), (1, 0)):
            for t in range(0, TRACERS, 2):
                for h in range(2):
                    both = [ref[h, t + k, pl.ds(8 + 64 * g + lon, 8, stride=LON)] for k in range(2)]
                    both = jnp.concatenate(both, axis=0).astype(jnp.bfloat16)
                    rim_out[s, side, pl.ds(RIM_ROWS * g + 8 * t, 16), HALF * h : HALF * (h + 1)] = both
        for c in rim_copies(s, g):
            c.start()

    def early_events():
        for e in range(EARLY):
            event(e)

    @pl.when(rank == 0)
    def _():
        early_events()

    def zrim_west(r):
        return tile_copy(zrim_out, zrim_in.at[r], zrim_send.at[0], zrim_recv.at[r], west)

    def zrim_round(r, k):
        return pltpu.make_async_remote_copy(
            src_ref=zrim_in.at[r], dst_ref=zrim_in.at[r], send_sem=zrim_send.at[k], recv_sem=zrim_recv.at[r],
            device_id={"trc": lax.rem(rank + k, GROUP)}, device_id_type=MESH,
        )

    @pl.when(rank < STEPS)
    def _():
        own.wait()
        for h in range(2):
            cols = slice(HALF * h, HALF * (h + 1))
            zonal_f[h] = zonal_own[:, cols].astype(jnp.float32)
            for g in range(LEV // 16):
                value = [zonal_f[h, pl.ds(128 * g + 64 * k, 8, stride=LON)] for k in range(2)]
                zrim_out[pl.ds(16 * g, 16), cols] = jnp.concatenate(value, axis=0).astype(jnp.bfloat16)

    for r in range(STEPS):
        @pl.when(rank == r)
        def _():
            zrim_west(r).start()

    for c in first:
        c.wait()
    for g in range(GROUPS):
        send_rims(0, g, cur_a)

    @pl.when(rank != 0)
    def _():
        early_events()

    def zrims_round():
        for r in range(STEPS):
            @pl.when(rank == r)
            def _():
                zrim_west(r).wait_recv()
                for k in range(1, GROUP):
                    zrim_round(r, k).start()

    def make_masks():
        for c in wet_copies:
            c.wait()
        depth_w, depth_e = wet_in[0, 7:8], wet_in[1, 0:1]
        depth_f = depth.astype(jnp.float32)
        beyond_w = jnp.where(row_a == 0, depth_w, pltpu.roll(depth_f, 1, 0))
        beyond_e = jnp.where(row_a == LON - 1, depth_e, pltpu.roll(depth_f, LON - 1, 0))
        beyond_s = jnp.where(lane == 0, 0.0, pltpu.roll(depth_f, 1, 1))
        beyond_n = jnp.where(lane == LAT - 1, 0.0, pltpu.roll(depth_f, LAT - 1, 1))
        for i, beyond in enumerate((beyond_w, beyond_e, beyond_s, beyond_n)):
            masks[i] = jnp.minimum(depth_f, beyond)
        masks[4] = depth_f

    def work(s, j, source, target):
        low, high = batch(j)
        before = 0 if j == 0 else (2 * low - 1) // 8 + 1
        for g in range(before, (2 * high - 1) // 8 + 1):
            for c in rim_copies(s, g):
                c.wait_recv()
            for side in range(2):
                rows = pl.ds(RIM_ROWS * g, RIM_ROWS)
                halo[side, rows] = rim_in[s, side, rows].astype(jnp.float32)

        def pair(p, _):
            start = pl.multiple_of(16 * p, 16)
            after = pl.multiple_of(16 * p + 16, 16)
            level3 = (level_of + 2 * p).astype(jnp.float32)
            level2 = level3[:2]

            def field(f, at):
                return rec[s, f, pl.ds(at, 16)].astype(jnp.float32).reshape(2, LON, LAT)

            def two_sided(courant, mask):
                plus = jnp.maximum(courant, 0.0) + DIFFUSION
                wet = mask[None] > level2
                return jnp.where(wet, plus, 0.0), jnp.where(wet, plus - courant, 0.0)

            zonal = field(0, start)
            zonal_e = pltpu.roll(zonal, LON - 1, 1)
            rims = [jnp.broadcast_to(zrim[pl.ds(2 * p + k, 1)], (LON, LAT)) for k in range(2)]
            zonal_e = jnp.where(row == LON - 1, jnp.stack(rims), zonal_e)
            from_w, to_w = two_sided(zonal, masks[0])
            to_e, from_e = two_sided(zonal_e, masks[1])
            merid = field(1, start)
            from_s, to_s = two_sided(merid, masks[2])
            to_n, from_n = two_sided(pltpu.roll(merid, LAT - 1, 2), masks[3])
            upward = jnp.concatenate([field(2, start), field(2, after)[:1]], axis=0)
            mixing = MIX_SCALE * jnp.abs(jnp.concatenate([field(3, start), field(3, after)[:1]], axis=0))
            wet3 = jnp.logical_and(masks[4][None] > level3, level3 > 0.0)
            plus3 = jnp.maximum(upward, 0.0) + mixing
            lower = jnp.where(wet3, plus3, 0.0)
            upper = jnp.where(wet3, plus3 - upward, 0.0)
            from_below, to_above = lower[1:], lower[:2]
            from_above, to_below = upper[:2], upper[1:]
            stay = 1.0 - (to_w + to_e + to_s + to_n + to_above + to_below)

            at = (p // 4) * RIM_ROWS + (p % 4) * 2
            for t in range(TRACERS):
                four = jnp.concatenate([source[h, t, pl.ds(start, 32)] for h in range(2)], axis=1).reshape(4, LON, LAT)
                here = four[1:3]
                side_w = jnp.stack([jnp.broadcast_to(halo[0, pl.ds(at + (8 * t + k), 1)], (LON, LAT)) for k in range(2)])
                side_e = jnp.stack([jnp.broadcast_to(halo[1, pl.ds(at + (8 * t + k), 1)], (LON, LAT)) for k in range(2)])
                at_w = jnp.where(row == 0, side_w, pltpu.roll(here, 1, 1))
                at_e = jnp.where(row == LON - 1, side_e, pltpu.roll(here, LON - 1, 1))
                new = stay * here + from_w * at_w + from_e * at_e
                new += from_s * pltpu.roll(here, 1, 2) + from_n * pltpu.roll(here, LAT - 1, 2)
                new += from_below * four[2:4] + from_above * four[0:2]
                new = new.reshape(16, LAT)
                for h in range(2):
                    target[h, t, pl.ds(pl.multiple_of(start + 8, 8), 16)] = new[:, HALF * h : HALF * (h + 1)]
            return 0

        lax.fori_loop(low, high, pair, 0)
        if s < STEPS - 1:
            for g in range(2 * low // 8, 2 * high // 8):
                send_rims(s + 1, g, target)

    done = EARLY
    stores = []
    for s in range(STEPS):
        source, target = ((cur_a, cur_b), (cur_b, cur_a))[s % 2]
        for j in range(SLABS):
            upto = READY[s][j]
            if s < STEPS - 1 or j < SLABS - 1:
                upto = min(len(EVENTS), upto + AHEAD)
            for e in range(done, upto):
                if e == RELAY:
                    zrims_round()
                event(e)
            done = max(done, upto)
            if j == 0 and s == 0:
                make_masks()
            if j == 0:
                @pl.when(rank != s)
                def _():
                    zrim_west(s).wait_recv()
                zrim[...] = zrim_in[s].astype(jnp.float32)
            work(s, j, source, target)
            if s == STEPS - 1:
                low, high = batch(j)
                count = 16 * (high - low)
                for h in range(2):
                    c = pltpu.make_async_copy(
                        target.at[h, :, pl.ds(8 + 16 * low, count)],
                        out.at[:, pl.ds(16 * low, count), pl.ds(HALF * h, HALF)],
                        store_sem.at[j, h],
                    )
                    c.start()
                    stores.append(c)

    for s in range(STEPS):
        for g in range(GROUPS):
            for c in rim_copies(s, g):
                c.wait_send()
    for r in range(STEPS):
        @pl.when(rank == r)
        def _():
            zrim_west(r).wait_send()
            for k in range(1, GROUP):
                zrim_round(r, k).wait_send()
    for e in range(len(EVENTS)):
        p, dirs = event_parts(e)
        for d in range(len(WAYS)):
            if any((v >> d) & 1 for v in EVENTS[e]):
                @pl.when((dirs // (1 << d)) % 2 == 1)
                def _():
                    hand_on(p, d).wait_send()
    for c in stores:
        c.wait()


def per_device(tracers, archive, sea_mask, levels):
    any_space = pl.BlockSpec(memory_space=pl.ANY)
    in_hbm = pl.BlockSpec(memory_space=pltpu.HBM)
    dma = pltpu.SemaphoreType.DMA
    result = pl.pallas_call(
        kernel,
        out_shape=jax.ShapeDtypeStruct((TRACERS, ROWS, LAT), jnp.float32),
        in_specs=[in_hbm, in_hbm, in_hbm, in_hbm],
        out_specs=any_space,
        scratch_shapes=[
            pltpu.VMEM((2, TRACERS, ROWS + 16, HALF), jnp.float32),
            pltpu.VMEM((2, TRACERS, ROWS + 16, HALF), jnp.float32),
            pltpu.VMEM((STEPS, 4, ROWS + 16, LAT), jnp.bfloat16),
            pltpu.VMEM((STEPS, 2, ROWS, LAT), jnp.bfloat16),
            pltpu.VMEM((STEPS, 2, ROWS, LAT), jnp.bfloat16),
            pltpu.VMEM((2, ROWS, LAT), jnp.float32),
            pltpu.VMEM((2, ROWS, HALF), jnp.float32),
            pltpu.VMEM((5, LON, LAT), jnp.float32),
            pltpu.VMEM((ROWS, LAT), jnp.bfloat16),
            pltpu.VMEM((LEV, LAT), jnp.bfloat16),
            pltpu.VMEM((STEPS, LEV, LAT), jnp.bfloat16),
            pltpu.VMEM((LEV, LAT), jnp.float32),
            pltpu.VMEM((LON, LAT), jnp.float32),
            pltpu.VMEM((2, LON, LAT), jnp.float32),
            pltpu.VMEM((LON, LAT), jnp.int32),
            pltpu.VMEM((LON, LAT), jnp.int32),
            dma((5,)),
            dma((STEPS * PIECES, len(WAYS))),
            dma((STEPS * PIECES,)),
            dma((STEPS, 2, GROUPS)),
            dma((STEPS, 2, GROUPS)),
            dma((GROUP,)),
            dma((STEPS,)),
            dma((2,)),
            dma((2,)),
            dma((SLABS, 2)),
        ],
        compiler_params=pltpu.CompilerParams(
            collective_id=0, has_side_effects=True, vmem_limit_bytes=VMEM_LIMIT
        ),
    )(
        tracers.reshape(TRACERS, ROWS, LAT),
        archive.reshape(4, ROWS, LAT),
        sea_mask,
        levels,
    )
    return result.reshape(TRACERS, LEV, LON, LAT)


def solution(mesh):
    in_specs = (
        P("trc", None, "tile", None),
        P("trc", None, None, "tile", None),
        P("tile", None),
        P("tile", None),
    )
    return jax.shard_map(
        per_device, mesh=mesh, in_specs=in_specs, out_specs=P("trc", None, "tile", None), check_vma=False
    )
```

time: 62.3 us -> 57.2 us (0.918); the launches traced: 62.1 us -> 56.3 us
  Pallas kernels: 57.8 us -> 52.1 us
    pallas_call x1, Pallas kernels: 57.8 us -> 52.1 us  [per_device(): pl.pallas_call(kernel, out_shape=jax.ShapeDtypeStruct((TRACERS, ROWS, LAT...]
where the time goes in v2:
time: 57.2 us; the launch traced here: 56.3 us
  Pallas kernels  52.1 us (91%)
  local copies, waits for them, and re-layouts  4.19 us (7%)
    pallas_call x1, Pallas kernels, per_device(): pl.pallas_call(kernel, out_shape=jax.ShapeDtypeStruct((TRACERS, ROWS, LAT...  52.1 us
    unnamed x7, local copies, waits for them, and re-layouts  4.19 us

profile of v2, /device:TPU:32, one launch (start us, length us, event | category | flops | bytes accessed | tf_op | source)
XLA Modules:
  0.0 56.3 jit_solution(1834089390895457094)
XLA Ops:
  0.0 0.0 copy-start
  0.0 1.1 %copy-done = bf16[1,4,48,8,256]{4,3,2,1,0:T(8,128)(2,1)S(1)} copy-done((bf16[1,4,48,8,256]{4,3,2,1,0:T(8,128)(2,1)S(1)}, bf16[1,4,48,8,256]{4,3,2,1,0:T(8,128)(2,1)}, u32[]{:S(2)}) %copy-start) | copy-done | bytes 786456
  1.1 0.0 copy-start.1
  1.1 0.7 %copy-done.1 = s32[8,256]{1,0:T(8,128)S(1)} copy-done((s32[8,256]{1,0:T(8,128)S(1)}, s32[8,256]{1,0:T(8,128)}, u32[]{:S(2)}) %copy-start.1) | copy-done | bytes 8216
  1.8 0.0 copy-start.2
  1.8 0.7 %copy-done.2 = s32[8,256]{1,0:T(8,128)S(1)} copy-done((s32[8,256]{1,0:T(8,128)S(1)}, s32[8,256]{1,0:T(8,128)}, u32[]{:S(2)}) %copy-start.2) | copy-done | bytes 8216
  2.5 52.1 %shard_map.46 = f32[8,384,256]{2,1,0:T(8,128)S(1)} custom-call(f32[8,384,256]{2,1,0:T(8,128)} %bitcast.5, bf16[4,384,256]{2,1,0:T(8,128)(2,1)S(1)} %bitcast.4, s32[8,256]{1,0:T(8,128)S(1)} %copy-done.1, s32[8,256]{1,0:T(8,128)S(1)} %copy-done.2), custom_call_target="tpu_custom_call" | custom-call | tf_op jit(solution)/shard_map/pallas_call | solution.py:395
  54.7 1.7 %copy.6 = f32[8,48,8,256]{3,2,1,0:T(8,128)} copy(f32[8,48,8,256]{3,2,1,0:T(8,128)S(1)} %bitcast.3) | data formatting | bytes 6291456
Async XLA Ops:
  0.0 1.1 %copy-start = (bf16[1,4,48,8,256]{4,3,2,1,0:T(8,128)(2,1)S(1)}, bf16[1,4,48,8,256]{4,3,2,1,0:T(8,128)(2,1)}, u32[]{:S(2)}) copy-start(bf16[1,4,48,8,256]{4,3,2,1,0:T(8,128)(2,1)} %param.5) | copy-start | bytes 2359300
  1.1 0.7 %copy-start.1 = (s32[8,256]{1,0:T(8,128)S(1)}, s32[8,256]{1,0:T(8,128)}, u32[]{:S(2)}) copy-start(s32[8,256]{1,0:T(8,128)} %sea_mask_hbm.1) | copy-start | bytes 24580
  1.8 0.7 %copy-start.2 = (s32[8,256]{1,0:T(8,128)S(1)}, s32[8,256]{1,0:T(8,128)}, u32[]{:S(2)}) copy-start(s32[8,256]{1,0:T(8,128)} %levels_hbm.1) | copy-start | bytes 24580

commit v3 on v2

--- a/solution.py
+++ b/solution.py
@@ -55,11 +55,11 @@
     (2816, 1280, 2816, 4352, 2816, 1280, 2945, 4352),
     (2944, 1408, 2944, 4480, 2944, 1408, 4480, 4480),
 )
-READY = ((19, 23, 27, 31, 34, 36), (22, 26, 30, 32, 34, 36), (15, 21, 27, 31, 34, 36))
-SLABS = 6
-AHEAD = 1
+READY = ((16, 19, 21, 23, 25, 27, 29, 31, 33, 34, 35, 36), (19, 22, 24, 26, 28, 30, 31, 32, 33, 34, 35, 36), (12, 15, 18, 21, 24, 27, 29, 31, 33, 34, 35, 36))
+SLABS = 12
+AHEAD = 0
 WAYS = ((1, 0), (3, 0), (0, 1), (2, 0), (1, 1), (3, 1), (2, 1))
-PIECES = SLABS * 2
+PIECES = SLABS
 SLAB_ROWS = ROWS // SLABS
 SLAB_PAIRS = PAIRS // SLABS
 EARLY = 6
@@ -102,20 +102,19 @@
     ]
     own = pltpu.make_async_copy(archive.at[0], zonal_own, load_sem.at[1])
 
-    def piece_ref(ref, record, half, slab):
+    def piece_ref(ref, record, slab):
         rows = pl.ds(pl.multiple_of(slab * SLAB_ROWS, SLAB_ROWS), SLAB_ROWS)
         if record is None:
-            return ref.at[pl.ds(2 * half, 2), rows]
-        return ref.at[record, pl.ds(2 * half, 2), rows]
+            return ref.at[:, rows]
+        return ref.at[record, :, rows]
 
     for r in range(STEPS):
         @pl.when(rank == r)
         def _():
             for j in range(SLABS):
-                for h in range(2):
-                    pltpu.make_async_copy(
-                        piece_ref(archive, None, h, j), piece_ref(rec, r, h, j), piece_recv.at[r * PIECES + 2 * j + h]
-                    ).start()
+                pltpu.make_async_copy(
+                    piece_ref(archive, None, j), piece_ref(rec, r, j), piece_recv.at[r * PIECES + j]
+                ).start()
 
     @pl.when(rank < STEPS)
     def _():
@@ -173,7 +172,7 @@
         return code // 128, code % 128
 
     def hand_on(p, d):
-        ref = piece_ref(rec, p // PIECES, p % 2, (p % PIECES) // 2)
+        ref = piece_ref(rec, p // PIECES, p % PIECES)
         return pltpu.make_async_remote_copy(
             src_ref=ref, dst_ref=ref, send_sem=piece_send.at[p, d], recv_sem=piece_recv.at[p],
             device_id={"trc": beside[d]}, device_id_type=MESH,
@@ -181,7 +180,7 @@
 
     def event(e):
         p, dirs = event_parts(e)
-        ref = piece_ref(rec, p // PIECES, p % 2, (p % PIECES) // 2)
+        ref = piece_ref(rec, p // PIECES, p % PIECES)
         pltpu.make_async_copy(ref, ref, piece_recv.at[p]).wait()
         for d in range(len(WAYS)):
             if any((v >> d) & 1 for v in EVENTS[e]):

time: 57.2 us -> 57 us (level); the launches traced: 56.3 us -> 56.8 us
  no operation moved by 1% of the time
where the time goes in v3:
time: 57 us; the launch traced here: 56.8 us
  Pallas kernels  52.6 us (92%)
  local copies, waits for them, and re-layouts  4.19 us (7%)
    pallas_call x1, Pallas kernels, per_device(): pl.pallas_call(kernel, out_shape=jax.ShapeDtypeStruct((TRACERS, ROWS, LAT...  52.6 us
    unnamed x7, local copies, waits for them, and re-layouts  4.19 us

profile of v3, /device:TPU:32, one launch (start us, length us, event | category | flops | bytes accessed | tf_op | source)
XLA Modules:
  0.0 56.8 jit_solution(2883627262405189235)
XLA Ops:
  0.0 0.0 copy-start
  0.0 1.1 %copy-done = bf16[1,4,48,8,256]{4,3,2,1,0:T(8,128)(2,1)S(1)} copy-done((bf16[1,4,48,8,256]{4,3,2,1,0:T(8,128)(2,1)S(1)}, bf16[1,4,48,8,256]{4,3,2,1,0:T(8,128)(2,1)}, u32[]{:S(2)}) %copy-start) | copy-done | bytes 786456
  1.1 0.0 copy-start.1
  1.1 0.7 %copy-done.1 = s32[8,256]{1,0:T(8,128)S(1)} copy-done((s32[8,256]{1,0:T(8,128)S(1)}, s32[8,256]{1,0:T(8,128)}, u32[]{:S(2)}) %copy-start.1) | copy-done | bytes 8216
  1.8 0.0 copy-start.2
  1.8 0.7 %copy-done.2 = s32[8,256]{1,0:T(8,128)S(1)} copy-done((s32[8,256]{1,0:T(8,128)S(1)}, s32[8,256]{1,0:T(8,128)}, u32[]{:S(2)}) %copy-start.2) | copy-done | bytes 8216
  2.5 52.6 %shard_map.46 = f32[8,384,256]{2,1,0:T(8,128)S(1)} custom-call(f32[8,384,256]{2,1,0:T(8,128)} %bitcast.5, bf16[4,384,256]{2,1,0:T(8,128)(2,1)S(1)} %bitcast.4, s32[8,256]{1,0:T(8,128)S(1)} %copy-done.1, s32[8,256]{1,0:T(8,128)S(1)} %copy-done.2), custom_call_target="tpu_custom_call" | custom-call | tf_op jit(solution)/shard_map/pallas_call | solution.py:394
  55.1 1.7 %copy.6 = f32[8,48,8,256]{3,2,1,0:T(8,128)} copy(f32[8,48,8,256]{3,2,1,0:T(8,128)S(1)} %bitcast.3) | data formatting | bytes 6291456
Async XLA Ops:
  0.0 1.1 %copy-start = (bf16[1,4,48,8,256]{4,3,2,1,0:T(8,128)(2,1)S(1)}, bf16[1,4,48,8,256]{4,3,2,1,0:T(8,128)(2,1)}, u32[]{:S(2)}) copy-start(bf16[1,4,48,8,256]{4,3,2,1,0:T(8,128)(2,1)} %param.5) | copy-start | bytes 2359300
  1.1 0.7 %copy-start.1 = (s32[8,256]{1,0:T(8,128)S(1)}, s32[8,256]{1,0:T(8,128)}, u32[]{:S(2)}) copy-start(s32[8,256]{1,0:T(8,128)} %sea_mask_hbm.1) | copy-start | bytes 24580
  1.8 0.7 %copy-start.2 = (s32[8,256]{1,0:T(8,128)S(1)}, s32[8,256]{1,0:T(8,128)}, u32[]{:S(2)}) copy-start(s32[8,256]{1,0:T(8,128)} %levels_hbm.1) | copy-start | bytes 24580
